TPU v7x, 32 devices: a whole 2x2x4 slice. The times are simulated.
32 devices in a mesh: row: 8 (over y, x, core), col: 4 (over z).
Axes of the slice: x: 2, y: 2, z: 4, core: 2. Of those that a mesh axis runs over, the one named last changes fastest.
Arguments:
- blocks: float32 [8, 4, 4, 8, 2, 64, 128], P('row', 'col'), may hold values from 0.5 to 1620
- plan: int32 [8, 4, 4, 8, 2], P('row', 'col'), may hold values from 0 to 511, as said below
- live: int32 [8, 4, 4, 8], P('row', 'col'), may hold values from 1 to 2, as said below
- row_emb: float32 [300, 8192], P(None, ('row', 'col')), may hold values from -1.5 to 1.5
- col_emb: float32 [300, 16384], P(None, ('col', 'row')), may hold values from -1.5 to 1.5
- row_acc: float32 [300, 8192], P(None, ('row', 'col')), may hold values from 0.5 to 5
- col_acc: float32 [300, 16384], P(None, ('col', 'row')), may hold values from 0.5 to 5
Outputs:
- new_row_emb: float32 [300, 8192], P(None, ('row', 'col'))
- new_col_emb: float32 [300, 16384], P(None, ('col', 'row'))
- new_row_acc: float32 [300, 8192], P(None, ('row', 'col'))
- new_col_acc: float32 [300, 16384], P(None, ('col', 'row'))
Inputs may be any that keep to these rules, and one draw needn't show every extreme that they name: plan[r, c, c2, r2, p] is a sub-block number of tile (r, c); numbers may repeat and repeated slots add. Over all index pairs (r2, c2), slot 0 names every sub-block row and every sub-block column of each tile. Slots at or past live[r, c, c2, r2] hold values that are not counts. In every draw some tile gets 2 live slots from every index pair.
All inputs are finite; a program needn't handle non-finite values.
Results may differ from a plain program's by a relative error of at most 0.0003.
Values sent between devices are 32-bit elements; how exact they have to be, the bound alone decides.
A program may use at most 192 MiB of HBM per device.

v0:
```python
import jax
import jax.numpy as jnp
from jax import lax
from jax.sharding import PartitionSpec as P

LEARNING_RATE = 0.2


def per_device(blocks, plan, live, row_emb, col_emb, row_acc, col_acc):
    rows_count = lax.axis_size("row")
    cols_count = lax.axis_size("col")
    highest = lax.Precision.HIGHEST
    outgoing = blocks[0, 0]
    arrived = lax.all_to_all(
        lax.all_to_all(outgoing, "row", split_axis=1, concat_axis=1, tiled=True),
        "col",
        split_axis=0,
        concat_axis=0,
        tiled=True,
    )
    sub_rows = blocks.shape[5]
    sub_cols = blocks.shape[6]
    tile_rows = row_emb.shape[1] * cols_count
    tile_cols = col_emb.shape[1] * rows_count
    grid_row_count = tile_rows // sub_rows
    grid_column_count = tile_cols // sub_cols
    block_total = grid_row_count * grid_column_count
    places = plan[0, 0]
    limits = live[0, 0]
    slot_ids = lax.broadcasted_iota(jnp.int32, places.shape, 2)
    target = jnp.where(slot_ids < limits[:, :, None], places, block_total)
    flat_layout = arrived.reshape(-1, sub_rows * sub_cols)
    dense_block_matrix = jax.ops.segment_sum(
        flat_layout, target.reshape(-1), num_segments=block_total + 1
    )[:block_total]
    tile_counts = (
        dense_block_matrix.reshape(grid_row_count, grid_column_count, sub_rows, sub_cols)
        .transpose(0, 2, 1, 3)
        .reshape(tile_rows, tile_cols)
    )
    row_part = jnp.sum(tile_counts, axis=1)
    col_part = jnp.sum(tile_counts, axis=0)
    col_mass = lax.psum(col_part, "row")
    row_mass = lax.psum(row_part, "col")
    grand_total = lax.psum(jnp.sum(row_part), ("row", "col"))
    row_block = lax.all_gather(row_emb, "col", axis=1, tiled=True)
    col_block = lax.all_gather(col_emb, "row", axis=1, tiled=True)
    rows_all = tile_rows * rows_count
    cols_all = tile_cols * cols_count
    loss_scale = 4.0 * float(rows_all * cols_all) ** (-0.25)
    col_base = jnp.log(grand_total) - jnp.log(col_mass)[None, :]
    row_logs = jnp.log(row_mass)
    step_rows = min(512, tile_rows)
    col_term = jnp.zeros((col_block.shape[0], tile_cols), jnp.float32)
    row_pieces = []
    for start in range(0, tile_rows, step_rows):
        counts_part = tile_counts[start : start + step_rows]
        vectors_part = row_block[:, start : start + step_rows]
        scores = lax.dot_general(
            vectors_part, col_block, (((0,), (0,)), ((), ())), precision=highest
        )
        baseline = col_base - row_logs[start : start + step_rows][:, None]
        positive = counts_part > 0
        pmi_target = jnp.log(jnp.where(positive, counts_part, 1.0)) + baseline
        confidence = 0.1 + 0.25 * jnp.sqrt(counts_part)
        loss_grad = (
            jnp.where(
                positive, confidence * (scores - pmi_target), jax.nn.sigmoid(scores - baseline)
            )
            * loss_scale
        )
        row_pieces.append(
            lax.dot_general(col_block, loss_grad, (((1,), (1,)), ((), ())), precision=highest)
        )
        col_term = col_term + jnp.dot(vectors_part, loss_grad, precision=highest)
    row_term = jnp.concatenate(row_pieces, axis=1)
    row_share = lax.psum_scatter(row_term, "col", scatter_dimension=1, tiled=True)
    col_share = lax.psum_scatter(col_term, "row", scatter_dimension=1, tiled=True)
    new_row_acc = row_acc + row_share * row_share
    new_col_acc = col_acc + col_share * col_share
    new_row_emb = row_emb - LEARNING_RATE * row_share / jnp.sqrt(new_row_acc)
    new_col_emb = col_emb - LEARNING_RATE * col_share / jnp.sqrt(new_col_acc)
    return (new_row_emb, new_col_emb, new_row_acc, new_col_acc)


def solution(mesh):
    return jax.shard_map(
        per_device,
        mesh=mesh,
        in_specs=(
            P("row", "col", None, None, None, None, None),
            P("row", "col", None, None, None),
            P("row", "col", None, None),
            P(None, ("row", "col")),
            P(None, ("col", "row")),
            P(None, ("row", "col")),
            P(None, ("col", "row")),
        ),
        out_specs=(
            P(None, ("row", "col")),
            P(None, ("col", "row")),
            P(None, ("row", "col")),
            P(None, ("col", "row")),
        ),
        check_vma=False,
    )
```

profile of v0, /device:TPU:0, one launch (start us, length us, event | category | flops | bytes accessed | tf_op | source)
XLA Modules:
  0.0 407.7 jit_solution(3145541196087119434)
XLA Ops:
  7.2 0.0 all-gather.3.cloned.1.call-start
  7.2 0.7 all-gather.3.cloned.1.call-update
  7.9 0.0 copy-start.10
  7.9 0.0 copy-start.11
  7.9 3.2 copy.40
  11.1 5.2 %all-to-all-start = ((f32[4,8,2,64,128]{4,3,2,0,1:T(8,128)}), f32[4,8,2,64,128]{4,3,2,0,1:T(8,128)S(1)}, u32[]{:S(2)}, u32[]{:S(2)}) async-start(f32[4,8,2,64,128]{4,3,2,0,1:T(8,128)} %bitcast.71), calls=%async_computation | async-start | bytes 4194304 | tf_op jit(solution)/shard_map/all_to_all | solution.py:15
  16.3 0.0 all-gather.5.cloned.1.call-start
  16.3 0.7 all-gather.5.cloned.1.call-update
  17.0 25.9 %all-to-all-done = f32[4,8,2,64,128]{4,3,2,0,1:T(8,128)S(1)} async-done(((f32[4,8,2,64,128]{4,3,2,0,1:T(8,128)}), f32[4,8,2,64,128]{4,3,2,0,1:T(8,128)S(1)}, u32[]{:S(2)}, u32[]{:S(2)}) %all-to-all-start) | async-done | bytes 2097184 | tf_op jit(solution)/shard_map/all_to_all | solution.py:15
  42.9 1.5 copy.26
  44.4 4.9 %all-to-all-start.1 = ((f32[4,8,2,64,128]{4,3,2,1,0:T(8,128)}), f32[4,8,2,64,128]{4,3,2,1,0:T(8,128)S(1)}, u32[]{:S(2)}, u32[]{:S(2)}) async-start(f32[4,8,2,64,128]{4,3,2,1,0:T(8,128)} %copy.26), calls=%async_computation.1 | async-start | bytes 4194304 | tf_op jit(solution)/shard_map/all_to_all | solution.py:14
  49.3 0.1 copy.24
  49.4 0.1 squeeze.6
  49.5 0.1 iota_compare_fusion
  49.6 0.1 lt.23
  49.7 45.0 %all-to-all-done.1 = f32[4,8,2,64,128]{4,3,2,1,0:T(8,128)S(1)} async-done(((f32[4,8,2,64,128]{4,3,2,1,0:T(8,128)}), f32[4,8,2,64,128]{4,3,2,1,0:T(8,128)S(1)}, u32[]{:S(2)}, u32[]{:S(2)}) %all-to-all-start.1) | async-done | bytes 2097184 | tf_op jit(solution)/shard_map/all_to_all | solution.py:14
  94.7 11.0 %scatter_custom_fusion = f32[513,8192]{1,0:T(8,128)} fusion(s32[64]{0:T(128)S(1)} %select_bitcast_fusion, f32[]{:T(128)} %constant.7.clone.1, f32[8,8,64,128]{3,2,1,0:T(8,128)S(1)} %bitcast.72), kind=kCustom, calls=%fused_computation.12 | custom fusion | flops 524288 | bytes 18907140 | tf_op jit(solution)/shard_map/scatter-add | solution.py:33
  105.7 13.2 %slice_reduce_fusion = (f32[]{:T(128)}, f32[64,8,64,128]{3,1,2,0:T(8,128)}) fusion(f32[513,8192]{1,0:T(8,128)} %scatter_custom_fusion), kind=kLoop, calls=%fused_computation.2 | loop fusion | flops 4194303 | bytes 33554436 | tf_op jit(solution)/shard_map/reduce_sum | solution.py:45
  119.0 39.5 %psum.21 = f32[]{:T(128)} all-reduce(f32[]{:T(128)} %get-tuple-element.10), channel_id=1, replica_groups=mesh['row'=8,'col'=4] {'row','col'}, use_global_device_ids=true, to_apply=%region_2.3 | all-reduce | flops 1 | bytes 8 | tf_op jit(solution)/shard_map/psum | solution.py:45
  158.5 14.1 %copy.30 = f32[64,8,64,128]{3,2,1,0:T(8,128)} copy(f32[64,8,64,128]{3,1,2,0:T(8,128)} %get-tuple-element.11) | data formatting | bytes 33554432
  173.3 8.5 %fusion.31 = (f32[32,128]{1,0:T(8,128)S(1)}, f32[16,64]{1,0:T(8,128)S(1)}) fusion(f32[16,32,64,128]{3,2,1,0:T(8,128)} %bitcast.67), kind=kLoop, calls=%fused_computation.57 | loop fusion | flops 8383488 | bytes 16797696 | tf_op jit(solution)/shard_map/reduce_sum | solution.py:42
  181.7 0.1 reduce_sum.35
  181.8 11.2 %psum.23 = f32[1024]{0:T(1024)S(1)} all-reduce(f32[1024]{0:T(1024)S(1)} %reduce_sum.35), channel_id=1, replica_groups=mesh['row'=8,'col'=4] {'col'}, use_global_device_ids=true, to_apply=%region_6.7 | all-reduce | flops 1024 | bytes 8192 | tf_op jit(solution)/shard_map/psum | solution.py:44
  193.0 6.6 %bitcast_bitcast_fusion = f32[16,64,32,128]{3,1,2,0:T(8,128)S(1)} fusion(f32[16,32,64,128]{3,2,1,0:T(8,128)} %bitcast.68), kind=kLoop, calls=%fused_computation.1 | loop fusion | bytes 33554432 | tf_op jit(solution)/shard_map/transpose | solution.py:38
  199.5 6.6 %fusion.32 = (f32[8,64,32,128]{3,1,2,0:T(8,128)}, f32[8,64,32,128]{3,1,2,0:T(8,128)}) fusion(f32[16,64,32,128]{3,1,2,0:T(8,128)S(1)} %bitcast_bitcast_fusion), kind=kLoop, calls=%fused_computation.58 | loop fusion | bytes 33554432 | tf_op jit(solution)/shard_map/slice | solution.py:57
  206.2 11.5 %copy.27 = f32[8,64,32,128]{3,2,1,0:T(8,128)} copy(f32[8,64,32,128]{3,1,2,0:T(8,128)} %get-tuple-element.12) | data formatting | bytes 16777216 | tf_op jit(solution)/shard_map/slice | solution.py:57
  217.7 8.0 %copy.28 = f32[8,64,32,128]{3,2,1,0:T(8,128)} copy(f32[8,64,32,128]{3,1,2,0:T(8,128)S(1)} %copy-done.2) | data formatting | bytes 16777216 | tf_op jit(solution)/shard_map/slice | solution.py:57
  225.7 23.4 %psum.22 = f32[4096]{0:T(1024)S(1)} all-reduce(f32[4096]{0:T(1024)S(1)} %bitcast.73), channel_id=1, replica_groups=mesh['row'=8,'col'=4] {'row'}, use_global_device_ids=true, to_apply=%region_4.5 | all-reduce | flops 4096 | bytes 32768 | tf_op jit(solution)/shard_map/psum | solution.py:43
  249.1 0.0 all-gather.3.cloned.1.call-done
  249.2 0.0 all-gather.5.cloned.1.call-done
  249.2 22.2 %fusion.3 = f32[512,4096]{1,0:T(8,128)S(1)} fusion(f32[64,8,32,128]{3,2,1,0:T(8,128)} %bitcast.70, f32[512]{0:T(512)S(1)} %get-tuple-element.14, f32[4096]{0:T(1024)S(1)} %log_subtract_fusion, f32[300,4096]{1,0:T(8,128)} %all-gather.5.cloned.1.call-done, f32[300,1024]{1,0:T(8,128)} %all-gather.3.cloned.1.call-done), kind=kOutput, calls=%fused_computation.15 | convolution fusion | flops 7579107328 | bytes 22398976 | tf_op jit(solution)/shard_map/dot_general | solution.py:59
  271.4 8.6 %convolution_bitcast_fusion.1 = f32[300,512]{1,0:T(8,128)S(1)} fusion(f32[512,4096]{1,0:T(8,128)S(1)} %fusion.3, f32[300,4096]{1,0:T(8,128)S(1)} %copy-done.3), kind=kOutput, calls=%fused_computation.42 | convolution fusion | flops 7549747200 | bytes 13918208 | tf_op jit(solution)/shard_map/dot_general | solution.py:73
  280.1 23.4 %fusion.5 = f32[512,4096]{1,0:T(8,128)S(1)} fusion(f32[64,8,32,128]{3,2,1,0:T(8,128)S(1)} %bitcast.69, f32[512]{0:T(512)S(1)} %get-tuple-element.15, f32[4096]{0:T(1024)S(1)} %log_subtract_fusion, f32[300,4096]{1,0:T(8,128)S(1)} %copy-done.3, f32[300,1024]{1,0:T(8,128)S(1)} %copy-done.6), kind=kOutput, calls=%fused_computation.17 | convolution fusion | flops 7579107328 | bytes 22398976 | tf_op jit(solution)/shard_map/dot_general | solution.py:59
  303.5 8.6 %convolution_bitcast_fusion = f32[300,512]{1,0:T(8,128)S(1)} fusion(f32[512,4096]{1,0:T(8,128)S(1)} %fusion.5, f32[300,4096]{1,0:T(8,128)S(1)} %copy-done.3), kind=kOutput, calls=%fused_computation.41 | convolution fusion | flops 7549747200 | bytes 13918208 | tf_op jit(solution)/shard_map/dot_general | solution.py:73
  312.1 1.1 pad_maximum_fusion
  313.2 0.0 reduce-scatter.3.cloned.1.call-update
  313.3 0.0 reduce-scatter.5.cloned.1.call-start
  313.3 11.4 %fusion.27 = f32[4096,300]{0,1:T(8,128)S(1)} fusion(f32[512,4096]{1,0:T(8,128)} %copy-done.1, f32[300,1024]{1,0:T(8,128)S(1)} %copy-done.6), kind=kOutput, calls=%fused_computation.48 | convolution fusion | flops 7549747200 | bytes 13926400 | tf_op jit(solution)/shard_map/dot_general | solution.py:75
  324.7 0.0 copy-start.7
  324.8 0.0 copy-start.9
  324.8 0.0 copy-start.5
  324.8 0.0 copy-start.8
  324.8 12.9 %fusion.22 = f32[300,4096]{1,0:T(8,128)} fusion(f32[4096,300]{0,1:T(8,128)S(1)} %fusion.27, f32[512,4096]{1,0:T(8,128)} %copy-done, f32[300,1024]{1,0:T(8,128)S(1)} %copy-done.6), kind=kOutput, calls=%fused_computation.37 | convolution fusion | flops 7550976000 | bytes 18907136 | tf_op jit(solution)/shard_map/dot_general | solution.py:75
  337.7 0.0 reduce-scatter.5.cloned.1.call-update
  337.7 3.2 reduce-scatter.3.cloned.1.call-done
  340.9 1.8 multiply_subtract_fusion.1
  342.8 55.9 %reduce-scatter.5.cloned.1.call-done = f32[300,512]{1,0:T(8,128)} async-done(((f32[300,4096]{1,0:T(8,128)}), f32[300,512]{1,0:T(8,128)}) %reduce-scatter.5.cloned.1.call-update) | async-done | bytes 614416 | tf_op jit(solution)/shard_map/reduce_scatter | solution.py:78
  398.6 2.3 multiply_subtract_fusion
  (23 shorter events, 0.1 us)
Async XLA Ops:
  7.2 242.0 %all-gather.3.cloned.1.call-start = ((), (), s32[]{:S(2)}) async-start(), calls=%async_computation.4 | async-start | bytes 1556480 | tf_op jit(solution)/shard_map/all_gather | solution.py:46
  7.9 41.4 %copy-start.10 = (s32[1,1,4,8,2]{3,4,2,1,0:T(2,128)S(1)}, s32[1,1,4,8,2]{3,4,2,1,0:T(2,128)}, u32[]{:S(2)}) copy-start(s32[1,1,4,8,2]{3,4,2,1,0:T(2,128)} %param.8) | copy-start | bytes 772
  7.9 41.6 %copy-start.11 = (s32[1,1,4,8]{3,2,1,0:T(4,128)S(1)}, s32[1,1,4,8]{3,2,1,0:T(4,128)}, u32[]{:S(2)}) copy-start(s32[1,1,4,8]{3,2,1,0:T(4,128)} %param.9) | copy-start | bytes 388
  11.1 31.8 %all-to-all-start = ((f32[4,8,2,64,128]{4,3,2,0,1:T(8,128)}), f32[4,8,2,64,128]{4,3,2,0,1:T(8,128)S(1)}, u32[]{:S(2)}, u32[]{:S(2)}) async-start(f32[4,8,2,64,128]{4,3,2,0,1:T(8,128)} %bitcast.71), calls=%async_computation | async-start | bytes 4194304 | tf_op jit(solution)/shard_map/all_to_all | solution.py:15
  16.3 232.9 %all-gather.5.cloned.1.call-start = ((), (), s32[]{:S(2)}) async-start(), calls=%async_computation.5 | async-start | bytes 5603328 | tf_op jit(solution)/shard_map/all_gather | solution.py:47
  44.4 50.3 %all-to-all-start.1 = ((f32[4,8,2,64,128]{4,3,2,1,0:T(8,128)}), f32[4,8,2,64,128]{4,3,2,1,0:T(8,128)S(1)}, u32[]{:S(2)}, u32[]{:S(2)}) async-start(f32[4,8,2,64,128]{4,3,2,1,0:T(8,128)} %copy.26), calls=%async_computation.1 | async-start | bytes 4194304 | tf_op jit(solution)/shard_map/all_to_all | solution.py:14
  49.3 291.6 %reduce-scatter.3.cloned.1.call-start = ((), (), s32[]{:S(2)}) async-start(), calls=%async_computation.6 | async-start | bytes 1556480 | tf_op jit(solution)/shard_map/reduce_scatter | solution.py:77
  206.2 11.5 %copy-start.2 = (f32[8,64,32,128]{3,1,2,0:T(8,128)S(1)}, f32[8,64,32,128]{3,1,2,0:T(8,128)}, u32[]{:S(2)}) copy-start(f32[8,64,32,128]{3,1,2,0:T(8,128)} %get-tuple-element.13) | copy-start | bytes 25165828
  249.2 22.2 %copy-start.3 = (f32[300,4096]{1,0:T(8,128)S(1)}, f32[300,4096]{1,0:T(8,128)}, u32[]{:S(2)}) copy-start(f32[300,4096]{1,0:T(8,128)} %all-gather.5.cloned.1.call-done) | copy-start | bytes 14745604
  271.4 8.6 %copy-start.1 = (f32[512,4096]{1,0:T(8,128)}, f32[512,4096]{1,0:T(8,128)S(1)}, u32[]{:S(2)}) copy-start(f32[512,4096]{1,0:T(8,128)S(1)} %fusion.3) | copy-start | bytes 25165828
  271.4 8.6 %copy-start.4 = (f32[8,64,32,128]{3,2,1,0:T(8,128)S(1)}, f32[8,64,32,128]{3,2,1,0:T(8,128)}, u32[]{:S(2)}) copy-start(f32[8,64,32,128]{3,2,1,0:T(8,128)} %copy.28) | copy-start | bytes 25165828
  271.4 8.6 %copy-start.6 = (f32[300,1024]{1,0:T(8,128)S(1)}, f32[300,1024]{1,0:T(8,128)}, u32[]{:S(2)}) copy-start(f32[300,1024]{1,0:T(8,128)} %all-gather.3.cloned.1.call-done) | copy-start | bytes 3686404
  303.5 8.6 %copy-start = (f32[512,4096]{1,0:T(8,128)}, f32[512,4096]{1,0:T(8,128)S(1)}, u32[]{:S(2)}) copy-start(f32[512,4096]{1,0:T(8,128)S(1)} %fusion.5) | copy-start | bytes 25165828
  313.3 85.4 %reduce-scatter.5.cloned.1.call-start = ((), (), s32[]{:S(2)}) async-start(), calls=%async_computation.7 | async-start | bytes 5603328 | tf_op jit(solution)/shard_map/reduce_scatter | solution.py:78
  324.7 16.2 %copy-start.7 = (f32[300,256]{1,0:T(8,128)S(1)}, f32[300,256]{1,0:T(8,128)}, u32[]{:S(2)}) copy-start(f32[300,256]{1,0:T(8,128)} %param.10) | copy-start | bytes 921604
  324.8 16.2 %copy-start.9 = (f32[300,256]{1,0:T(8,128)S(1)}, f32[300,256]{1,0:T(8,128)}, u32[]{:S(2)}) copy-start(f32[300,256]{1,0:T(8,128)} %param.12) | copy-start | bytes 921604
  324.8 73.9 %copy-start.5 = (f32[300,512]{1,0:T(8,128)S(1)}, f32[300,512]{1,0:T(8,128)}, u32[]{:S(2)}) copy-start(f32[300,512]{1,0:T(8,128)} %param.11) | copy-start | bytes 1843204
  324.8 73.9 %copy-start.8 = (f32[300,512]{1,0:T(8,128)S(1)}, f32[300,512]{1,0:T(8,128)}, u32[]{:S(2)}) copy-start(f32[300,512]{1,0:T(8,128)} %param.13) | copy-start | bytes 1843204
Sparse Core Ops, SparseCore 0:
  9.6 34.2 all-gather.2
  45.8 39.0 all-gather.4
  313.4 27.4 reduce-scatter.2
  344.7 53.8 reduce-scatter.4
where the time goes:
time: 414 us; the launch traced here: 408 us
  waiting for transfers between devices  131 us (32%)
  matrix products  87.1 us (21%)
  blocking collectives  74.1 us (18%)
  local copies, waits for them, and re-layouts  51.9 us (13%)
  other arithmetic  38.1 us (9%)
  between operations  14.9 us (4%)
  starting transfers between devices  10.2 us (2%)
    reduce_scatter x1, waiting for transfers between devices, per_device(): lax.psum_scatter(col_term, 'row', scatter_dimension=1, tiled=True)  55.9 us
    dot_general x2, matrix products, per_device(): lax.dot_general(vectors_part, col_block, (((0,), (0,)), ((), ())), precis...  45.6 us
    all_to_all x1, waiting for transfers between devices, per_device(): lax.all_to_all(lax.all_to_all(outgoing, 'row', split_axis=1, concat_axis=...  45 us
    psum x1, blocking collectives, per_device(): grand_total = lax.psum(jnp.sum(row_part), ('row', 'col'))  39.5 us
    slice x3, local copies, waits for them, and re-layouts, per_device(): counts_part = tile_counts[start:start + step_rows]  26.1 us
    all_to_all x1, waiting for transfers between devices, per_device(): lax.all_to_all(outgoing, 'row', split_axis=1, concat_axis=1, tiled=True)  25.9 us
    dot_general x2, matrix products, per_device(): col_term = col_term + jnp.dot(vectors_part, loss_grad, precision=highest)  24.3 us
    psum x1, blocking collectives, per_device(): col_mass = lax.psum(col_part, 'row')  23.4 us
  transfers between devices with their start and end apart: 6, of which 4 were waited for; matrix products, arithmetic and copies ran while one was open for 27% of the time, Pallas kernels for 0%

commit v1 on v0

v1 whole, which is shorter than its diff:
```python
import functools

import jax
import jax.numpy as jnp
from jax import lax
from jax.experimental import pallas as pl
from jax.experimental.pallas import tpu as pltpu
from jax.sharding import PartitionSpec as P

LEARNING_RATE = 0.2
MESH = pl.DeviceIdType.MESH
VMEM_LIMIT = 56 * 1024 * 1024


def round_up(value, step):
    return -(-value // step) * step


def remote(src, dst, send_sem, recv_sem, device):
    return pltpu.make_async_remote_copy(
        src_ref=src, dst_ref=dst, send_sem=send_sem, recv_sem=recv_sem,
        device_id=device, device_id_type=MESH,
    )


def exchange_kernel(
    n_row, n_col, blocks, row_emb, col_emb, arrived, rows, cols,
    a_send, a_recv, r_send, r_recv, c_send, c_recv, f_send, f_recv, local_sem,
):
    r = lax.axis_index("row")
    c = lax.axis_index("col")
    core = lax.rem(r, 2)
    sibling = r + 1 - 2 * core
    chips = n_row // 2
    total = n_row * n_col

    def peer(k):
        return lax.rem(r + k % n_row, n_row), lax.rem(c + k // n_row, n_col)

    def chip_peer(t):
        return lax.rem(r + 2 * t, n_row)

    barrier = pltpu.get_barrier_semaphore()

    @pl.loop(1, total)
    def _(k):
        pl.semaphore_signal(barrier, inc=1, device_id=peer(k), device_id_type=MESH)

    pl.semaphore_wait(barrier, total - 1)

    local = [
        pltpu.make_async_copy(blocks.at[c, r], arrived.at[c, r], local_sem.at[0]),
        pltpu.make_async_copy(row_emb, rows.at[c], local_sem.at[1]),
        pltpu.make_async_copy(col_emb, cols.at[r], local_sem.at[2]),
    ]

    def row_copy(k):
        return remote(row_emb, rows.at[c], r_send.at[k], r_recv.at[k], (r, lax.rem(c + k, n_col)))

    def col_copy(t):
        return remote(col_emb, cols.at[r], c_send.at[t], c_recv.at[t], (chip_peer(t), c))

    def pair_copy():
        return remote(col_emb, cols.at[r], f_send.at[0], f_recv.at[0], (sibling, c))

    def forward(t):
        origin = lax.rem(r + n_row - 2 * t, n_row)
        return remote(cols.at[origin], cols.at[origin], f_send.at[t], f_recv.at[t], (sibling, c))

    def block_copy(k):
        pr, pc = peer(k)
        return remote(blocks.at[pc, pr], arrived.at[c, r], a_send.at[k], a_recv.at[k], (pr, pc))

    @pl.loop(1, chips)
    def _(t):
        col_copy(t).start()

    pair_copy().start()

    @pl.loop(1, total)
    def _(k):
        block_copy(total - k).start()

    @pl.loop(1, n_col)
    def _(k):
        row_copy(k).start()

    for copy in local:
        copy.start()

    @pl.loop(1, chips)
    def _(t):
        col_copy(t).wait_recv()
        forward(t).start()

    for copy in local:
        copy.wait()
    pair_copy().wait()

    @pl.loop(1, chips)
    def _(t):
        col_copy(t).wait_send()
        forward(t).wait()

    @pl.loop(1, n_col)
    def _(k):
        row_copy(k).wait()

    @pl.loop(1, total)
    def _(k):
        block_copy(k).wait()


def exchange(n_row, n_col, blocks, row_emb, col_emb):
    f32 = jnp.float32
    any_spec = pl.BlockSpec(memory_space=pl.ANY)
    dma = pltpu.SemaphoreType.DMA
    total = n_row * n_col
    return pl.pallas_call(
        functools.partial(exchange_kernel, n_row, n_col),
        out_shape=(
            jax.ShapeDtypeStruct(blocks.shape, f32),
            jax.ShapeDtypeStruct((n_col,) + row_emb.shape, f32),
            jax.ShapeDtypeStruct((n_row,) + col_emb.shape, f32),
        ),
        in_specs=[any_spec] * 3,
        out_specs=(any_spec,) * 3,
        scratch_shapes=[
            dma((total,)), dma((total,)), dma((n_col,)), dma((n_col,)),
            dma((n_row // 2,)), dma((n_row // 2,)), dma((n_row // 2,)), dma((n_row // 2,)), dma((3,)),
        ],
        compiler_params=pltpu.CompilerParams(collective_id=0, has_side_effects=True),
        name="exchange",
    )(blocks, row_emb, col_emb)


def merge_kernel(scale, plan, live, blocks, gain, offset, table, row_part, col_part, row_sum, seen):
    slots, sub_rows, sub_cols = blocks.shape
    places = table.shape[0]
    grid_columns = col_part.shape[0]

    @pl.loop(0, places)
    def _(b):
        table[b] = slots

    row_sum[...] = jnp.zeros_like(row_sum)
    col_part[...] = jnp.zeros_like(col_part)
    gain[slots] = jnp.zeros((sub_rows, sub_cols), jnp.float32)
    offset[slots] = jnp.zeros((sub_rows, sub_cols), jnp.float32)

    @pl.loop(0, slots)
    def _(k):
        @pl.when(live[k] > 0)
        def _():
            place = plan[k]
            i = place // grid_columns
            j = place - i * grid_columns
            block = blocks[k]
            row_sum[i] = row_sum[i] + block
            col_part[pl.ds(j, 1), :] += jnp.sum(block, axis=0, keepdims=True)
            first = table[place]
            fresh = first == slots
            target = jnp.where(fresh, k, first)
            table[place] = target

            @pl.when(fresh)
            def _():
                seen[k] = block

            @pl.when(jnp.logical_not(fresh))
            def _():
                seen[target] = seen[target] + block
                seen[k] = block

        @pl.when(live[k] <= 0)
        def _():
            seen[k] = jnp.ones((sub_rows, sub_cols), jnp.float32)

    @pl.loop(0, slots)
    def _(k):
        counts = seen[k]
        confidence = scale * (0.1 + 0.25 * jnp.sqrt(counts))
        gain[k] = confidence
        offset[k] = -confidence * jnp.log(counts)

    row_part[...] = jnp.sum(row_sum[...], axis=2)


def merge(scale, plan, live, blocks, grid_rows, grid_columns):
    slots, sub_rows, sub_cols = blocks.shape
    f32 = jnp.float32
    smem = pl.BlockSpec(memory_space=pltpu.SMEM)
    vmem = pl.BlockSpec(memory_space=pltpu.VMEM)
    return pl.pallas_call(
        functools.partial(merge_kernel, scale),
        out_shape=(
            jax.ShapeDtypeStruct((slots + 1, sub_rows, sub_cols), f32),
            jax.ShapeDtypeStruct((slots + 1, sub_rows, sub_cols), f32),
            jax.ShapeDtypeStruct((grid_rows * grid_columns,), jnp.int32),
            jax.ShapeDtypeStruct((grid_rows, sub_rows), f32),
            jax.ShapeDtypeStruct((grid_columns, sub_cols), f32),
        ),
        in_specs=[smem, smem, vmem],
        out_specs=(vmem, vmem, smem, vmem, vmem),
        scratch_shapes=[
            pltpu.VMEM((grid_rows, sub_rows, sub_cols), f32),
            pltpu.VMEM((slots, sub_rows, sub_cols), f32),
        ],
        compiler_params=pltpu.CompilerParams(vmem_limit_bytes=VMEM_LIMIT),
        name="merge",
    )(plan, live, blocks)


def mass_kernel(
    n_row, n_col, row_part, col_part, row_log, col_log, row_in, col_in, tot_out, tot_in,
    r_send, r_recv, c_send, c_recv, t_send, t_recv,
):
    r = lax.axis_index("row")
    c = lax.axis_index("col")

    def row_peer(k):
        return (lax.rem(r + k, n_row), c)

    def col_peer(k):
        return (r, lax.rem(c + k, n_col))

    barrier = pltpu.get_barrier_semaphore()

    @pl.loop(1, n_row)
    def _(k):
        pl.semaphore_signal(barrier, inc=1, device_id=row_peer(k), device_id_type=MESH)

    @pl.loop(1, n_col)
    def _(k):
        pl.semaphore_signal(barrier, inc=1, device_id=col_peer(k), device_id_type=MESH)

    pl.semaphore_wait(barrier, n_row + n_col - 2)

    def col_copy(k):
        return remote(col_part, col_in.at[k], c_send.at[k], c_recv.at[k], row_peer(k))

    def row_copy(k):
        return remote(row_part, row_in.at[k], r_send.at[k], r_recv.at[k], col_peer(k))

    def tot_copy(k):
        return remote(tot_out, tot_in.at[k], t_send.at[k], t_recv.at[k], col_peer(k))

    @pl.loop(1, n_row)
    def _(k):
        col_copy(k).start()

    @pl.loop(1, n_col)
    def _(k):
        row_copy(k).start()

    @pl.loop(1, n_row)
    def _(k):
        col_copy(k).wait()

    col_mass = col_part[...]
    for k in range(1, n_row):
        col_mass = col_mass + col_in[k]
    part = jnp.sum(jnp.sum(col_mass, axis=0, keepdims=True), axis=1, keepdims=True)
    tot_out[...] = jnp.broadcast_to(part, tot_out.shape)

    @pl.loop(1, n_col)
    def _(k):
        tot_copy(k).start()

    @pl.loop(1, n_col)
    def _(k):
        row_copy(k).wait()

    row_mass = row_part[...]
    for k in range(1, n_col):
        row_mass = row_mass + row_in[k]
    row_log[...] = jnp.log(row_mass)

    @pl.loop(1, n_col)
    def _(k):
        tot_copy(k).wait()

    grand = tot_out[...]
    for k in range(1, n_col):
        grand = grand + tot_in[k]
    col_log[...] = jnp.log(col_mass) - jnp.log(grand[0:1, :])


def masses(n_row, n_col, row_part, col_part):
    f32 = jnp.float32
    vmem = pl.BlockSpec(memory_space=pltpu.VMEM)
    dma = pltpu.SemaphoreType.DMA
    return pl.pallas_call(
        functools.partial(mass_kernel, n_row, n_col),
        out_shape=(
            jax.ShapeDtypeStruct(row_part.shape, f32),
            jax.ShapeDtypeStruct(col_part.shape, f32),
        ),
        in_specs=[vmem] * 2,
        out_specs=(vmem,) * 2,
        scratch_shapes=[
            pltpu.VMEM((n_col,) + row_part.shape, f32),
            pltpu.VMEM((n_row,) + col_part.shape, f32),
            pltpu.VMEM((8, col_part.shape[1]), f32),
            pltpu.VMEM((n_col, 8, col_part.shape[1]), f32),
            dma((n_col,)), dma((n_col,)), dma((n_row,)), dma((n_row,)), dma((n_col,)), dma((n_col,)),
        ],
        compiler_params=pltpu.CompilerParams(collective_id=1, has_side_effects=True),
        name="masses",
    )(row_part, col_part)


def gradient_kernel(
    n_row, n_col, dim, dim_pad, depth, half_scale,
    table, rows, cols, gain, offset, row_log, col_log, row_share, col_share,
    pad_row, pad_col, row_left, row_turned, col_right, lg_hi, lg_lo, row_sum, col_out, pair_in, chip_in, row_in,
    p_send, p_recv, h_send, h_recv, r_send, r_recv,
):
    f32 = jnp.float32
    bf16 = jnp.bfloat16
    r = lax.axis_index("row")
    c = lax.axis_index("col")
    core = lax.rem(r, 2)
    chip = r // 2
    chips = n_row // 2
    sibling = r + 1 - 2 * core
    row_width = rows.shape[2]
    col_width = cols.shape[2]
    sub_rows, sub_cols = gain.shape[1:]
    per_chunk = col_width // sub_cols
    grid_columns = col_log.shape[0]

    barrier = pltpu.get_barrier_semaphore()
    pl.semaphore_signal(barrier, inc=1, device_id=(sibling, c), device_id_type=MESH)

    @pl.loop(1, chips)
    def _(t):
        pl.semaphore_signal(barrier, inc=1, device_id=(lax.rem(r + 2 * t, n_row), c), device_id_type=MESH)

    @pl.loop(1, n_col)
    def _(k):
        pl.semaphore_signal(barrier, inc=1, device_id=(r, lax.rem(c + k, n_col)), device_id_type=MESH)

    pl.semaphore_wait(barrier, chips + n_col - 1)

    def pair_copy(t):
        return remote(col_out.at[2 * t], pair_in.at[t], p_send.at[t], p_recv.at[t], (sibling, c))

    def chip_copy(t):
        return remote(
            col_out.at[2 * t + 1], chip_in.at[t], h_send.at[t], h_recv.at[t],
            (lax.rem(r + 2 * (t + 1), n_row), c),
        )

    def row_copy(k):
        target = lax.rem(c + k, n_col)
        return remote(row_sum.at[target], row_in.at[k], r_send.at[k], r_recv.at[k], (r, target))

    pad_row[...] = jnp.zeros_like(pad_row)
    pad_col[...] = jnp.zeros_like(pad_col)
    row_left[...] = jnp.zeros_like(row_left)
    col_right[...] = jnp.zeros_like(col_right)
    row_sum[...] = jnp.zeros_like(row_sum)
    for q in range(n_col):
        pad_row[0:dim, :] = rows[q]
        value = pad_row[...]
        high = value.astype(bf16)
        low = (value - high.astype(f32)).astype(bf16)
        span = slice(q * row_width, (q + 1) * row_width)
        row_left[0:dim_pad, span] = high
        row_left[dim_pad : 2 * dim_pad, span] = low
        row_left[2 * dim_pad : 3 * dim_pad, span] = high
        row_turned[span, :] = row_left[:, span].T

    @pl.loop(0, 2 * chips)
    def _(step):
        t = step // 2
        second = step % 2
        chunk = 2 * lax.rem(chip + 1 + t, chips) + jnp.where(second == 1, core, 1 - core)
        pad_col[0:dim, :] = cols[chunk]
        value = pad_col[...]
        high = value.astype(bf16)
        low = (value - high.astype(f32)).astype(bf16)
        col_right[0:dim_pad, :] = high
        col_right[dim_pad : 2 * dim_pad, :] = high
        col_right[2 * dim_pad : 3 * dim_pad, :] = low

        @pl.loop(0, n_col)
        def _(q):
            base = pl.multiple_of(q * row_width, row_width)
            scores = jnp.dot(row_turned[pl.ds(base, row_width), :], col_right[...], preferred_element_type=f32)
            strips = []
            for j in range(per_chunk):
                column = chunk * per_chunk + j
                col_base = col_log[pl.ds(column, 1), :]
                pieces = []
                for i in range(row_width // sub_rows):
                    line = q * (row_width // sub_rows) + i
                    slot = table[line * grid_columns + column]
                    a = gain[slot]
                    b = offset[slot]
                    row_base = row_log[pl.ds(pl.multiple_of(line * sub_rows, sub_rows), sub_rows), :]
                    x = (
                        scores[i * sub_rows : (i + 1) * sub_rows, j * sub_cols : (j + 1) * sub_cols]
                        + row_base + col_base
                    )
                    pieces.append(jnp.where(a > 0, a * x + b, half_scale + half_scale * jnp.tanh(0.5 * x)))
                strips.append(jnp.concatenate(pieces, axis=0))
            slope = jnp.concatenate(strips, axis=1)
            high = slope.astype(bf16)
            low = (slope - high.astype(f32)).astype(bf16)
            lg_hi[pl.ds(base, row_width), :] = high
            lg_lo[pl.ds(base, row_width), :] = low
            dims = (((1,), (1,)), ((), ()))
            both = lax.dot_general(
                col_right[dim_pad : 3 * dim_pad, :], high, dims, preferred_element_type=f32
            )
            rest = lax.dot_general(col_right[0:dim_pad, :], low, dims, preferred_element_type=f32)
            row_sum[q] = row_sum[q] + (both[0:dim_pad] + (both[dim_pad:] + rest))

        @pl.when(step == 2 * chips - 1)
        def _():
            @pl.loop(1, n_col)
            def _(k):
                row_copy(k).start()

        both = jnp.dot(row_left[0 : 2 * dim_pad, :], lg_hi[...], preferred_element_type=f32)
        rest = jnp.dot(row_left[0:dim_pad, :], lg_lo[...], preferred_element_type=f32)
        col_out[step] = both[0:dim_pad] + (both[dim_pad:] + rest)

        @pl.when(second == 0)
        def _():
            pair_copy(t).start()

        @pl.when(second == 1)
        def _():
            pair_copy(t).wait_recv()
            col_out[step] = col_out[step] + pair_in[t]

            @pl.when(t < chips - 1)
            def _():
                chip_copy(t).start()

    total = col_out[2 * chips - 1]
    for t in range(chips - 1):
        chip_copy(t).wait_recv()
        total = total + chip_in[t]
    col_share[...] = total[0:dim]
    row_total = row_sum[c]
    for k in range(1, n_col):
        row_copy(k).wait_recv()
        row_total = row_total + row_in[k]
    row_share[...] = row_total[0:dim]

    @pl.loop(0, chips)
    def _(t):
        pair_copy(t).wait_send()

    @pl.loop(0, chips - 1)
    def _(t):
        chip_copy(t).wait_send()

    @pl.loop(1, n_col)
    def _(k):
        row_copy(k).wait_send()


def gradients(n_row, n_col, half_scale, table, rows, cols, gain, offset, row_log, col_log):
    f32 = jnp.float32
    bf16 = jnp.bfloat16
    dim, row_width = rows.shape[1:]
    col_width = cols.shape[2]
    dim_pad = round_up(dim, 16)
    depth = round_up(3 * dim_pad, 128)
    tile_rows = n_col * row_width
    chips = n_row // 2
    smem = pl.BlockSpec(memory_space=pltpu.SMEM)
    vmem = pl.BlockSpec(memory_space=pltpu.VMEM)
    dma = pltpu.SemaphoreType.DMA
    return pl.pallas_call(
        functools.partial(gradient_kernel, n_row, n_col, dim, dim_pad, depth, half_scale),
        out_shape=(
            jax.ShapeDtypeStruct((dim, row_width), f32),
            jax.ShapeDtypeStruct((dim, col_width), f32),
        ),
        in_specs=[smem] + [vmem] * 6,
        out_specs=(vmem,) * 2,
        scratch_shapes=[
            pltpu.VMEM((dim_pad, row_width), f32),
            pltpu.VMEM((dim_pad, col_width), f32),
            pltpu.VMEM((depth, tile_rows), bf16),
            pltpu.VMEM((tile_rows, depth), bf16),
            pltpu.VMEM((depth, col_width), bf16),
            pltpu.VMEM((tile_rows, col_width), bf16),
            pltpu.VMEM((tile_rows, col_width), bf16),
            pltpu.VMEM((n_col, dim_pad, row_width), f32),
            pltpu.VMEM((2 * chips, dim_pad, col_width), f32),
            pltpu.VMEM((chips, dim_pad, col_width), f32),
            pltpu.VMEM((max(chips - 1, 1), dim_pad, col_width), f32),
            pltpu.VMEM((n_col, dim_pad, row_width), f32),
            dma((chips,)), dma((chips,)), dma((chips,)), dma((chips,)), dma((n_col,)), dma((n_col,)),
        ],
        compiler_params=pltpu.CompilerParams(
            collective_id=2, has_side_effects=True, vmem_limit_bytes=VMEM_LIMIT
        ),
        name="gradients",
    )(table, rows, cols, gain, offset, row_log, col_log)


def per_device(blocks, plan, live, row_emb, col_emb, row_acc, col_acc):
    n_row = lax.axis_size("row")
    n_col = lax.axis_size("col")
    sub_rows, sub_cols = blocks.shape[5:]
    tile_rows = row_emb.shape[1] * n_col
    tile_cols = col_emb.shape[1] * n_row
    scale = 4.0 * float(tile_rows * n_row * tile_cols * n_col) ** (-0.25)
    arrived, rows, cols = exchange(n_row, n_col, blocks[0, 0], row_emb, col_emb)
    places = plan[0, 0]
    slot_ids = lax.broadcasted_iota(jnp.int32, places.shape, 2)
    alive = (slot_ids < live[0, 0][:, :, None]).astype(jnp.int32)
    gain, offset, table, row_part, col_part = merge(
        scale, places.reshape(-1), alive.reshape(-1), arrived.reshape(-1, sub_rows, sub_cols),
        tile_rows // sub_rows, tile_cols // sub_cols,
    )
    row_log, col_log = masses(n_row, n_col, row_part, col_part)
    row_wide = jnp.broadcast_to(row_log.reshape(tile_rows, 1), (tile_rows, sub_cols))
    row_share, col_share = gradients(
        n_row, n_col, 0.5 * scale, table, rows, cols, gain, offset, row_wide, col_log
    )
    new_row_acc = row_acc + row_share * row_share
    new_col_acc = col_acc + col_share * col_share
    new_row_emb = row_emb - LEARNING_RATE * row_share / jnp.sqrt(new_row_acc)
    new_col_emb = col_emb - LEARNING_RATE * col_share / jnp.sqrt(new_col_acc)
    return (new_row_emb, new_col_emb, new_row_acc, new_col_acc)


def solution(mesh):
    return jax.shard_map(
        per_device,
        mesh=mesh,
        in_specs=(
            P("row", "col", None, None, None, None, None),
            P("row", "col", None, None, None),
            P("row", "col", None, None),
            P(None, ("row", "col")),
            P(None, ("col", "row")),
            P(None, ("row", "col")),
            P(None, ("col", "row")),
        ),
        out_specs=(
            P(None, ("row", "col")),
            P(None, ("col", "row")),
            P(None, ("row", "col")),
            P(None, ("col", "row")),
        ),
        check_vma=False,
    )
```

time: 414 us -> 192 us (0.46)
  Pallas kernels: 0 us -> 179 us
  waiting for transfers between devices: 131 us -> 0 us
  matrix products: 87.1 us -> 0 us
  blocking collectives: 74.1 us -> 0 us
  local copies, waits for them, and re-layouts: 51.9 us -> 3.82 us
  other arithmetic: 38.1 us -> 4.91 us
  between operations: 14.9 us -> 0.69 us
  starting transfers between devices: 10.2 us -> 0 us
    pallas_call x0 -> x4, Pallas kernels: none -> 179 us  [the longest x1 77 us: exchange(): pl.pallas_call(functools.partial(exchange_kernel, n_row, n_col), out_shap...]
    dot_general x6 -> x0, matrix products: 87.1 us -> none  [the longest x2 45.6 us: per_device(): lax.dot_general(vectors_part, col_block, (((0,), (0,)), ((), ())), precis...]
    psum x3 -> x0, blocking collectives: 74.1 us -> none  [the longest x1 39.5 us: per_device(): grand_total = lax.psum(jnp.sum(row_part), ('row', 'col'))]
    all_to_all x2 -> x0, waiting for transfers between devices: 70.9 us -> none  [the longest x1 45 us: per_device(): lax.all_to_all(lax.all_to_all(outgoing, 'row', split_axis=1, concat_axis=...]
    reduce_scatter x2 -> x0, waiting for transfers between devices: 59.1 us -> none  [the longest x1 55.9 us: per_device(): lax.psum_scatter(col_term, 'row', scatter_dimension=1, tiled=True)]
    slice x4 -> x0, local copies, waits for them, and re-layouts: 26.1 us -> none  [the longest x3 26.1 us: per_device(): counts_part = tile_counts[start:start + step_rows]]
    reduce_sum x2 -> x0, other arithmetic: 21.7 us -> none  [the longest x1 13.2 us: per_device(): grand_total = lax.psum(jnp.sum(row_part), ('row', 'col'))]
    unnamed x27 -> x9, local copies, waits for them, and re-layouts: 17.4 us -> 0.79 us
  transfers between devices with their start and end apart: 6 -> 0, of which waited for: 4 -> 0; matrix products, arithmetic and copies ran while one was open for 27% -> 0% of each run, Pallas kernels for 0% -> 0%
where the time goes in v1:
time: 192 us; the launch traced here: 188 us
  Pallas kernels  179 us (93%)
  other arithmetic  4.91 us (3%)
  local copies, waits for them, and re-layouts  3.82 us (2%)
    pallas_call x1, Pallas kernels, exchange(): pl.pallas_call(functools.partial(exchange_kernel, n_row, n_col), out_shap...  77 us
    pallas_call x1, Pallas kernels, gradients(): pl.pallas_call(functools.partial(gradient_kernel, n_row, n_col, dim, dim_...  70.9 us
    pallas_call x1, Pallas kernels, masses(): pl.pallas_call(functools.partial(mass_kernel, n_row, n_col), out_shape=(j...  19.8 us
    pallas_call x1, Pallas kernels, merge(): pl.pallas_call(functools.partial(merge_kernel, scale), out_shape=(jax.Sha...  10.9 us

profile of v1, /device:TPU:0, one launch (start us, length us, event | category | flops | bytes accessed | tf_op | source)
XLA Modules:
  0.0 188.0 jit_solution(9872587963739120017)
XLA Ops:
  0.6 0.8 copy.12
  1.4 0.6 reshape_squeeze.3.plan
  2.0 0.8 fusion
  2.8 0.6 reshape.21.live
  3.4 77.0 %exchange.1 = (f32[4,8,2,64,128]{4,3,2,1,0:T(8,128)}, f32[4,300,256]{2,1,0:T(8,128)}, f32[8,300,512]{2,1,0:T(8,128)}) custom-call(f32[4,8,2,64,128]{4,3,2,1,0:T(8,128)} %bitcast.5, f32[300,256]{1,0:T(8,128)} %row_emb.1, f32[300,512]{1,0:T(8,128)} %col_emb.1), custom_call_target="tpu_custom_call" | custom-call | tf_op jit(solution)/shard_map/exchange/pallas_call | solution.py:119
  80.5 10.9 %merge.1 = (f32[65,64,128]{2,1,0:T(8,128)}, f32[65,64,128]{2,1,0:T(8,128)}, s32[512]{0:T(512)}, f32[16,64]{1,0:T(8,128)}, f32[32,128]{1,0:T(8,128)}) custom-call(s32[64]{0:T(128)} %reshape_squeeze.3.plan, s32[64]{0:T(128)} %reshape.21.live, f32[64,64,128]{2,1,0:T(8,128)} %bitcast.6), custom_call_target="tpu_custom_call" | custom-call | tf_op jit(solution)/shard_map/merge/pallas_call | solution.py:194
  91.3 19.8 %masses.1 = (f32[16,64]{1,0:T(8,128)}, f32[32,128]{1,0:T(8,128)}) custom-call(f32[16,64]{1,0:T(8,128)} %get-tuple-element.22.row_part, f32[32,128]{1,0:T(8,128)} %get-tuple-element.23.col_part), custom_call_target="tpu_custom_call" | custom-call | tf_op jit(solution)/shard_map/masses/pallas_call | solution.py:293
  111.1 0.8 broadcast_in_dim.7
  111.9 1.0 broadcast_in_dim.8.row_log
  112.9 0.0 copy-start.1
  112.9 0.0 copy-start.3
  112.9 0.0 copy-start
  112.9 0.0 copy-start.2
  112.9 70.9 %gradients.1 = (f32[300,256]{1,0:T(8,128)}, f32[300,512]{1,0:T(8,128)}) custom-call(s32[512]{0:T(512)} %get-tuple-element.17.table, f32[4,300,256]{2,1,0:T(8,128)} %get-tuple-element.18.rows, f32[8,300,512]{2,1,0:T(8,128)} %get-tuple-element.19.cols, f32[65,64,128]{2,1,0:T(8,128)} %get-tuple-element.20.gain, f32[65,64,128]{2,1,0:T(8,128)} %get-tuple-element.21.offset, ...), custom_call_target="tpu_custom_call" | custom-call | tf_op jit(solution)/shard_map/gradients/pallas_call | solution.py:480
  183.8 0.0 copy-done.1
  183.8 0.0 copy-done.3
  183.8 1.9 multiply_subtract_fusion.1
  185.7 0.0 copy-done
  185.7 0.0 copy-done.2
  185.7 2.3 %multiply_subtract_fusion = (f32[300,512]{1,0:T(8,128)}, f32[300,512]{1,0:T(8,128)}) fusion(f32[300,512]{1,0:T(8,128)S(1)} %copy-done, f32[300,512]{1,0:T(8,128)} %get-tuple-element.27, f32[300,512]{1,0:T(8,128)S(1)} %copy-done.2), kind=kLoop, calls=%fused_computation | loop fusion | flops 768000 | bytes 3072000 | tf_op jit(solution)/shard_map/sub | solution.py:533
Async XLA Ops:
  112.9 70.9 %copy-start.1 = (f32[300,256]{1,0:T(8,128)S(1)}, f32[300,256]{1,0:T(8,128)}, u32[]{:S(2)}) copy-start(f32[300,256]{1,0:T(8,128)} %row_emb.1) | copy-start | bytes 921604
  112.9 70.9 %copy-start.3 = (f32[300,256]{1,0:T(8,128)S(1)}, f32[300,256]{1,0:T(8,128)}, u32[]{:S(2)}) copy-start(f32[300,256]{1,0:T(8,128)} %param.12) | copy-start | bytes 921604
  112.9 72.8 %copy-start = (f32[300,512]{1,0:T(8,128)S(1)}, f32[300,512]{1,0:T(8,128)}, u32[]{:S(2)}) copy-start(f32[300,512]{1,0:T(8,128)} %col_emb.1) | copy-start | bytes 1843204
  112.9 72.8 %copy-start.2 = (f32[300,512]{1,0:T(8,128)S(1)}, f32[300,512]{1,0:T(8,128)}, u32[]{:S(2)}) copy-start(f32[300,512]{1,0:T(8,128)} %param.13) | copy-start | bytes 1843204

commit v2 on v1

--- a/solution.py
+++ b/solution.py
@@ -25,7 +25,7 @@
 
 def exchange_kernel(
     n_row, n_col, blocks, row_emb, col_emb, arrived, rows, cols,
-    a_send, a_recv, r_send, r_recv, c_send, c_recv, f_send, f_recv, local_sem,
+    a_send, a_recv, r_send, r_recv, d_send, d_recv, c_send, c_recv, f_send, f_recv, local_sem,
 ):
     r = lax.axis_index("row")
     c = lax.axis_index("col")
@@ -54,8 +54,24 @@
         pltpu.make_async_copy(col_emb, cols.at[r], local_sem.at[2]),
     ]
 
-    def row_copy(k):
-        return remote(row_emb, rows.at[c], r_send.at[k], r_recv.at[k], (r, lax.rem(c + k, n_col)))
+    after = (r, lax.rem(c + 1, n_col))
+    before = (r, lax.rem(c + n_col - 1, n_col))
+
+    def up(k):
+        shard = lax.rem(c + n_col - k + 1, n_col)
+        source = row_emb if k == 1 else rows.at[shard]
+        return remote(source, rows.at[shard], r_send.at[k], r_recv.at[k], after)
+
+    def down(k):
+        shard = lax.rem(c + k - 1, n_col)
+        source = row_emb if k == 1 else rows.at[shard]
+        return remote(source, rows.at[shard], d_send.at[k], d_recv.at[k], before)
+
+    def sends_up(k):
+        return jnp.logical_and(c + 1 < n_col, c >= k - 1)
+
+    def sends_down(k):
+        return jnp.logical_and(c >= 1, c + k - 1 < n_col)
 
     def col_copy(t):
         return remote(col_emb, cols.at[r], c_send.at[t], c_recv.at[t], (chip_peer(t), c))
@@ -71,6 +87,14 @@
         pr, pc = peer(k)
         return remote(blocks.at[pc, pr], arrived.at[c, r], a_send.at[k], a_recv.at[k], (pr, pc))
 
+    @pl.when(sends_up(1))
+    def _():
+        up(1).start()
+
+    @pl.when(sends_down(1))
+    def _():
+        down(1).start()
+
     @pl.loop(1, chips)
     def _(t):
         col_copy(t).start()
@@ -81,12 +105,28 @@
     def _(k):
         block_copy(total - k).start()
 
-    @pl.loop(1, n_col)
-    def _(k):
-        row_copy(k).start()
-
     for copy in local:
         copy.start()
+
+    for k in range(1, n_col):
+
+        @pl.when(c >= k)
+        def _():
+            up(k).wait_recv()
+
+        @pl.when(c + k < n_col)
+        def _():
+            down(k).wait_recv()
+
+        if k + 1 < n_col:
+
+            @pl.when(sends_up(k + 1))
+            def _():
+                up(k + 1).start()
+
+            @pl.when(sends_down(k + 1))
+            def _():
+                down(k + 1).start()
 
     @pl.loop(1, chips)
     def _(t):
@@ -102,9 +142,15 @@
         col_copy(t).wait_send()
         forward(t).wait()
 
-    @pl.loop(1, n_col)
-    def _(k):
-        row_copy(k).wait()
+    for k in range(1, n_col):
+
+        @pl.when(sends_up(k))
+        def _():
+            up(k).wait_send()
+
+        @pl.when(sends_down(k))
+        def _():
+            down(k).wait_send()
 
     @pl.loop(1, total)
     def _(k):
@@ -126,7 +172,7 @@
         in_specs=[any_spec] * 3,
         out_specs=(any_spec,) * 3,
         scratch_shapes=[
-            dma((total,)), dma((total,)), dma((n_col,)), dma((n_col,)),
+            dma((total,)), dma((total,)), dma((n_col,)), dma((n_col,)), dma((n_col,)), dma((n_col,)),
             dma((n_row // 2,)), dma((n_row // 2,)), dma((n_row // 2,)), dma((n_row // 2,)), dma((3,)),
         ],
         compiler_params=pltpu.CompilerParams(collective_id=0, has_side_effects=True),
@@ -313,7 +359,8 @@
 def gradient_kernel(
     n_row, n_col, dim, dim_pad, depth, half_scale,
     table, rows, cols, gain, offset, row_log, col_log, row_share, col_share,
-    pad_row, pad_col, row_left, row_turned, col_right, lg_hi, lg_lo, row_sum, col_out, pair_in, chip_in, row_in,
+    pad_row, pad_col, row_left, row_turned, right_0, right_1, score_0, score_1, lg_hi, lg_lo,
+    row_sum, col_out, pair_in, chip_in, row_in,
     p_send, p_recv, h_send, h_recv, r_send, r_recv,
 ):
     f32 = jnp.float32
@@ -329,6 +376,9 @@
     sub_rows, sub_cols = gain.shape[1:]
     per_chunk = col_width // sub_cols
     grid_columns = col_log.shape[0]
+    halves, _, _, piece = row_sum.shape
+    lines = piece // sub_rows
+    shard_lines = row_width // sub_rows
 
     barrier = pltpu.get_barrier_semaphore()
     pl.semaphore_signal(barrier, inc=1, device_id=(sibling, c), device_id_type=MESH)
@@ -352,90 +402,114 @@
             (lax.rem(r + 2 * (t + 1), n_row), c),
         )
 
-    def row_copy(k):
+    def row_copy(h, k):
         target = lax.rem(c + k, n_col)
-        return remote(row_sum.at[target], row_in.at[k], r_send.at[k], r_recv.at[k], (r, target))
-
-    pad_row[...] = jnp.zeros_like(pad_row)
-    pad_col[...] = jnp.zeros_like(pad_col)
-    row_left[...] = jnp.zeros_like(row_left)
-    col_right[...] = jnp.zeros_like(col_right)
-    row_sum[...] = jnp.zeros_like(row_sum)
-    for q in range(n_col):
-        pad_row[0:dim, :] = rows[q]
-        value = pad_row[...]
+        sem = h * n_col + k
+        return remote(
+            row_sum.at[h, target], row_in.at[h, k], r_send.at[sem], r_recv.at[sem], (r, target)
+        )
+
+    def split(value):
         high = value.astype(bf16)
-        low = (value - high.astype(f32)).astype(bf16)
-        span = slice(q * row_width, (q + 1) * row_width)
-        row_left[0:dim_pad, span] = high
-        row_left[dim_pad : 2 * dim_pad, span] = low
-        row_left[2 * dim_pad : 3 * dim_pad, span] = high
-        row_turned[span, :] = row_left[:, span].T
-
-    @pl.loop(0, 2 * chips)
-    def _(step):
-        t = step // 2
-        second = step % 2
-        chunk = 2 * lax.rem(chip + 1 + t, chips) + jnp.where(second == 1, core, 1 - core)
-        pad_col[0:dim, :] = cols[chunk]
-        value = pad_col[...]
-        high = value.astype(bf16)
-        low = (value - high.astype(f32)).astype(bf16)
-        col_right[0:dim_pad, :] = high
-        col_right[dim_pad : 2 * dim_pad, :] = high
-        col_right[2 * dim_pad : 3 * dim_pad, :] = low
-
-        @pl.loop(0, n_col)
-        def _(q):
-            base = pl.multiple_of(q * row_width, row_width)
-            scores = jnp.dot(row_turned[pl.ds(base, row_width), :], col_right[...], preferred_element_type=f32)
-            strips = []
-            for j in range(per_chunk):
-                column = chunk * per_chunk + j
-                col_base = col_log[pl.ds(column, 1), :]
-                pieces = []
-                for i in range(row_width // sub_rows):
-                    line = q * (row_width // sub_rows) + i
+        return high, (value - high.astype(f32)).astype(bf16)
+
+    def chunk_at(u, second):
+        t = lax.rem(u, chips)
+        return 2 * lax.rem(chip + 1 + t, chips) + (core if second else 1 - core)
+
+    def prepare(u, second, right, score):
+        pad_col[0:dim, :] = cols[chunk_at(u, second)]
+        high, low = split(pad_col[...])
+        right[0:dim_pad, :] = high
+        right[dim_pad : 2 * dim_pad, :] = high
+        right[2 * dim_pad : 3 * dim_pad, :] = low
+        score[...] = jnp.dot(row_turned[u // chips], right[...], preferred_element_type=f32)
+
+    def work(u, second, right, score):
+        h = u // chips
+        chunk = chunk_at(u, second)
+        step = 2 * lax.rem(u, chips) + second
+        for j in range(per_chunk):
+            column = chunk * per_chunk + j
+            col_base = col_log[pl.ds(column, 1), :]
+            across = slice(j * sub_cols, (j + 1) * sub_cols)
+            for q in range(n_col):
+                values = []
+                for i in range(lines):
+                    line = q * shard_lines + h * lines + i
                     slot = table[line * grid_columns + column]
                     a = gain[slot]
                     b = offset[slot]
                     row_base = row_log[pl.ds(pl.multiple_of(line * sub_rows, sub_rows), sub_rows), :]
-                    x = (
-                        scores[i * sub_rows : (i + 1) * sub_rows, j * sub_cols : (j + 1) * sub_cols]
-                        + row_base + col_base
+                    at = q * piece + i * sub_rows
+                    x = score[at : at + sub_rows, across] + (row_base + col_base)
+                    values.append(
+                        jnp.where(a > 0, a * x + b, half_scale + half_scale * jnp.tanh(0.5 * x))
                     )
-                    pieces.append(jnp.where(a > 0, a * x + b, half_scale + half_scale * jnp.tanh(0.5 * x)))
-                strips.append(jnp.concatenate(pieces, axis=0))
-            slope = jnp.concatenate(strips, axis=1)
-            high = slope.astype(bf16)
-            low = (slope - high.astype(f32)).astype(bf16)
-            lg_hi[pl.ds(base, row_width), :] = high
-            lg_lo[pl.ds(base, row_width), :] = low
-            dims = (((1,), (1,)), ((), ()))
-            both = lax.dot_general(
-                col_right[dim_pad : 3 * dim_pad, :], high, dims, preferred_element_type=f32
-            )
-            rest = lax.dot_general(col_right[0:dim_pad, :], low, dims, preferred_element_type=f32)
-            row_sum[q] = row_sum[q] + (both[0:dim_pad] + (both[dim_pad:] + rest))
-
-        @pl.when(step == 2 * chips - 1)
+                high, low = split(jnp.concatenate(values, axis=0))
+                lg_hi[q * piece : (q + 1) * piece, across] = high
+                lg_lo[q * piece : (q + 1) * piece, across] = low
+        dims = (((1,), (1,)), ((), ()))
+        both = lax.dot_general(
+            right[dim_pad : 3 * dim_pad, :], lg_hi[...], dims, preferred_element_type=f32
+        )
+        rest = lax.dot_general(right[0:dim_pad, :], lg_lo[...], dims, preferred_element_type=f32)
+        row_new = both[0:dim_pad] + (both[dim_pad:] + rest)
+        for q in range(n_col):
+            row_sum[h, q] = row_sum[h, q] + row_new[:, q * piece : (q + 1) * piece]
+        left = row_left.at[h]
+        both = jnp.dot(left[0 : 2 * dim_pad, :], lg_hi[...], preferred_element_type=f32)
+        rest = jnp.dot(left[0:dim_pad, :], lg_lo[...], preferred_element_type=f32)
+        col_out[step] = col_out[step] + (both[0:dim_pad] + (both[dim_pad:] + rest))
+
+    pad_row[...] = jnp.zeros_like(pad_row)
+    pad_col[...] = jnp.zeros_like(pad_col)
+    row_left[...] = jnp.zeros_like(row_left)
+    right_0[...] = jnp.zeros_like(right_0)
+    right_1[...] = jnp.zeros_like(right_1)
+    row_sum[...] = jnp.zeros_like(row_sum)
+
+    @pl.loop(0, 2 * chips)
+    def _(step):
+        col_out[step] = jnp.zeros(col_out.shape[1:], f32)
+
+    for q in range(n_col):
+        pad_row[0:dim, :] = rows[q]
+        high, low = split(pad_row[...])
+        for h in range(halves):
+            span = slice(q * piece, (q + 1) * piece)
+            part = slice(h * piece, (h + 1) * piece)
+            row_left[h, 0:dim_pad, span] = high[:, part]
+            row_left[h, dim_pad : 2 * dim_pad, span] = low[:, part]
+            row_left[h, 2 * dim_pad : 3 * dim_pad, span] = high[:, part]
+            row_turned[h, span, :] = row_left[h, :, span].T
+
+    prepare(0, 0, right_0, score_0)
+
+    @pl.loop(0, halves * chips)
+    def _(u):
+        t = lax.rem(u, chips)
+        last = u >= (halves - 1) * chips
+        prepare(u, 1, right_1, score_1)
+        work(u, 0, right_0, score_0)
+
+        @pl.when(last)
+        def _():
+            pair_copy(t).start()
+
+        prepare(jnp.minimum(u + 1, halves * chips - 1), 0, right_0, score_0)
+        work(u, 1, right_1, score_1)
+
+        @pl.when(t == chips - 1)
         def _():
             @pl.loop(1, n_col)
             def _(k):
-                row_copy(k).start()
-
-        both = jnp.dot(row_left[0 : 2 * dim_pad, :], lg_hi[...], preferred_element_type=f32)
-        rest = jnp.dot(row_left[0:dim_pad, :], lg_lo[...], preferred_element_type=f32)
-        col_out[step] = both[0:dim_pad] + (both[dim_pad:] + rest)
-
-        @pl.when(second == 0)
-        def _():
-            pair_copy(t).start()
-
-        @pl.when(second == 1)
+                row_copy(u // chips, k).start()
+
+        @pl.when(last)
         def _():
             pair_copy(t).wait_recv()
-            col_out[step] = col_out[step] + pair_in[t]
+            col_out[2 * t + 1] = col_out[2 * t + 1] + pair_in[t]
 
             @pl.when(t < chips - 1)
             def _():
@@ -446,11 +520,12 @@
         chip_copy(t).wait_recv()
         total = total + chip_in[t]
     col_share[...] = total[0:dim]
-    row_total = row_sum[c]
-    for k in range(1, n_col):
-        row_copy(k).wait_recv()
-        row_total = row_total + row_in[k]
-    row_share[...] = row_total[0:dim]
+    for h in range(halves):
+        row_total = row_sum[h, c]
+        for k in range(1, n_col):
+            row_copy(h, k).wait_recv()
+            row_total = row_total + row_in[h, k]
+        row_share[:, h * piece : (h + 1) * piece] = row_total[0:dim]
 
     @pl.loop(0, chips)
     def _(t):
@@ -460,9 +535,11 @@
     def _(t):
         chip_copy(t).wait_send()
 
-    @pl.loop(1, n_col)
-    def _(k):
-        row_copy(k).wait_send()
+    for h in range(halves):
+
+        @pl.loop(1, n_col)
+        def _(k):
+            row_copy(h, k).wait_send()
 
 
 def gradients(n_row, n_col, half_scale, table, rows, cols, gain, offset, row_log, col_log):
@@ -472,7 +549,9 @@
     col_width = cols.shape[2]
     dim_pad = round_up(dim, 16)
     depth = round_up(3 * dim_pad, 128)
-    tile_rows = n_col * row_width
+    halves = 2 if row_width % 256 == 0 else 1
+    piece = row_width // halves
+    half_rows = n_col * piece
     chips = n_row // 2
     smem = pl.BlockSpec(memory_space=pltpu.SMEM)
     vmem = pl.BlockSpec(memory_space=pltpu.VMEM)
@@ -488,17 +567,21 @@
         scratch_shapes=[
             pltpu.VMEM((dim_pad, row_width), f32),
             pltpu.VMEM((dim_pad, col_width), f32),
-            pltpu.VMEM((depth, tile_rows), bf16),
-            pltpu.VMEM((tile_rows, depth), bf16),
+            pltpu.VMEM((halves, depth, half_rows), bf16),
+            pltpu.VMEM((halves, half_rows, depth), bf16),
             pltpu.VMEM((depth, col_width), bf16),
-            pltpu.VMEM((tile_rows, col_width), bf16),
-            pltpu.VMEM((tile_rows, col_width), bf16),
-            pltpu.VMEM((n_col, dim_pad, row_width), f32),
+            pltpu.VMEM((depth, col_width), bf16),
+            pltpu.VMEM((half_rows, col_width), f32),
+            pltpu.VMEM((half_rows, col_width), f32),
+            pltpu.VMEM((half_rows, col_width), bf16),
+            pltpu.VMEM((half_rows, col_width), bf16),
+            pltpu.VMEM((halves, n_col, dim_pad, piece), f32),
             pltpu.VMEM((2 * chips, dim_pad, col_width), f32),
             pltpu.VMEM((chips, dim_pad, col_width), f32),
             pltpu.VMEM((max(chips - 1, 1), dim_pad, col_width), f32),
-            pltpu.VMEM((n_col, dim_pad, row_width), f32),
-            dma((chips,)), dma((chips,)), dma((chips,)), dma((chips,)), dma((n_col,)), dma((n_col,)),
+            pltpu.VMEM((halves, n_col, dim_pad, piece), f32),
+            dma((chips,)), dma((chips,)), dma((chips,)), dma((chips,)),
+            dma((halves * n_col,)), dma((halves * n_col,)),
         ],
         compiler_params=pltpu.CompilerParams(
             collective_id=2, has_side_effects=True, vmem_limit_bytes=VMEM_LIMIT

time: 192 us -> 175 us (0.911)
  Pallas kernels: 179 us -> 163 us
    pallas_call x1, Pallas kernels: 70.9 us -> 58.5 us  [gradients(): pl.pallas_call(functools.partial(gradient_kernel, n_row, n_col, dim, dim_...]
    pallas_call x1, Pallas kernels: 19.8 us -> 12 us  [masses(): pl.pallas_call(functools.partial(mass_kernel, n_row, n_col), out_shape=(j...]
    pallas_call x1, Pallas kernels: 77 us -> 81.9 us  [exchange(): pl.pallas_call(functools.partial(exchange_kernel, n_row, n_col), out_shap...]
where the time goes in v2:
time: 175 us; the launch traced here: 173 us
  Pallas kernels  163 us (93%)
  other arithmetic  4.91 us (3%)
  local copies, waits for them, and re-layouts  3.82 us (2%)
    pallas_call x1, Pallas kernels, exchange(): pl.pallas_call(functools.partial(exchange_kernel, n_row, n_col), out_shap...  81.9 us
    pallas_call x1, Pallas kernels, gradients(): pl.pallas_call(functools.partial(gradient_kernel, n_row, n_col, dim, dim_...  58.5 us
    pallas_call x1, Pallas kernels, masses(): pl.pallas_call(functools.partial(mass_kernel, n_row, n_col), out_shape=(j...  12 us
    pallas_call x1, Pallas kernels, merge(): pl.pallas_call(functools.partial(merge_kernel, scale), out_shape=(jax.Sha...  10.9 us

profile of v2, /device:TPU:0, one launch (start us, length us, event | category | flops | bytes accessed | tf_op | source)
XLA Modules:
  0.0 172.7 jit_solution(9563259354308936839)
XLA Ops:
  0.6 0.8 copy.12
  1.4 0.6 reshape_squeeze.3.plan
  2.0 0.8 fusion
  2.8 0.6 reshape.21.live
  3.4 81.9 %exchange.1 = (f32[4,8,2,64,128]{4,3,2,1,0:T(8,128)}, f32[4,300,256]{2,1,0:T(8,128)}, f32[8,300,512]{2,1,0:T(8,128)}) custom-call(f32[4,8,2,64,128]{4,3,2,1,0:T(8,128)} %bitcast.5, f32[300,256]{1,0:T(8,128)} %row_emb.1, f32[300,512]{1,0:T(8,128)} %col_emb.1), custom_call_target="tpu_custom_call" | custom-call | tf_op jit(solution)/shard_map/exchange/pallas_call | solution.py:165
  85.3 10.9 %merge.1 = (f32[65,64,128]{2,1,0:T(8,128)}, f32[65,64,128]{2,1,0:T(8,128)}, s32[512]{0:T(512)}, f32[16,64]{1,0:T(8,128)}, f32[32,128]{1,0:T(8,128)}) custom-call(s32[64]{0:T(128)} %reshape_squeeze.3.plan, s32[64]{0:T(128)} %reshape.21.live, f32[64,64,128]{2,1,0:T(8,128)} %bitcast.6), custom_call_target="tpu_custom_call" | custom-call | tf_op jit(solution)/shard_map/merge/pallas_call | solution.py:240
  96.2 12.0 %masses.1 = (f32[16,64]{1,0:T(8,128)}, f32[32,128]{1,0:T(8,128)}) custom-call(f32[16,64]{1,0:T(8,128)} %get-tuple-element.22.row_part, f32[32,128]{1,0:T(8,128)} %get-tuple-element.23.col_part), custom_call_target="tpu_custom_call" | custom-call | tf_op jit(solution)/shard_map/masses/pallas_call | solution.py:339
  108.2 0.8 broadcast_in_dim.7
  109.0 1.0 broadcast_in_dim.8.row_log
  110.0 0.0 copy-start.1
  110.0 0.0 copy-start.3
  110.0 0.0 copy-start
  110.0 0.0 copy-start.2
  110.0 58.5 %gradients.1 = (f32[300,256]{1,0:T(8,128)}, f32[300,512]{1,0:T(8,128)}) custom-call(s32[512]{0:T(512)} %get-tuple-element.17.table, f32[4,300,256]{2,1,0:T(8,128)} %get-tuple-element.18.rows, f32[8,300,512]{2,1,0:T(8,128)} %get-tuple-element.19.cols, f32[65,64,128]{2,1,0:T(8,128)} %get-tuple-element.20.gain, f32[65,64,128]{2,1,0:T(8,128)} %get-tuple-element.21.offset, ...), custom_call_target="tpu_custom_call" | custom-call | tf_op jit(solution)/shard_map/gradients/pallas_call | solution.py:559
  168.5 0.0 copy-done.1
  168.5 0.0 copy-done.3
  168.6 1.9 %multiply_subtract_fusion.1 = (f32[300,256]{1,0:T(8,128)}, f32[300,256]{1,0:T(8,128)}) fusion(f32[300,256]{1,0:T(8,128)S(1)} %copy-done.1, f32[300,256]{1,0:T(8,128)} %get-tuple-element.26, f32[300,256]{1,0:T(8,128)S(1)} %copy-done.3), kind=kLoop, calls=%fused_computation.2 | loop fusion | flops 384000 | bytes 1536000 | tf_op jit(solution)/shard_map/sub | solution.py:615
  170.4 0.0 copy-done
  170.4 0.0 copy-done.2
  170.4 2.3 %multiply_subtract_fusion = (f32[300,512]{1,0:T(8,128)}, f32[300,512]{1,0:T(8,128)}) fusion(f32[300,512]{1,0:T(8,128)S(1)} %copy-done, f32[300,512]{1,0:T(8,128)} %get-tuple-element.27, f32[300,512]{1,0:T(8,128)S(1)} %copy-done.2), kind=kLoop, calls=%fused_computation | loop fusion | flops 768000 | bytes 3072000 | tf_op jit(solution)/shard_map/sub | solution.py:616
Async XLA Ops:
  110.0 58.6 %copy-start.1 = (f32[300,256]{1,0:T(8,128)S(1)}, f32[300,256]{1,0:T(8,128)}, u32[]{:S(2)}) copy-start(f32[300,256]{1,0:T(8,128)} %row_emb.1) | copy-start | bytes 921604
  110.0 58.6 %copy-start.3 = (f32[300,256]{1,0:T(8,128)S(1)}, f32[300,256]{1,0:T(8,128)}, u32[]{:S(2)}) copy-start(f32[300,256]{1,0:T(8,128)} %param.12) | copy-start | bytes 921604
  110.0 60.4 %copy-start = (f32[300,512]{1,0:T(8,128)S(1)}, f32[300,512]{1,0:T(8,128)}, u32[]{:S(2)}) copy-start(f32[300,512]{1,0:T(8,128)} %col_emb.1) | copy-start | bytes 1843204
  110.0 60.4 %copy-start.2 = (f32[300,512]{1,0:T(8,128)S(1)}, f32[300,512]{1,0:T(8,128)}, u32[]{:S(2)}) copy-start(f32[300,512]{1,0:T(8,128)} %param.13) | copy-start | bytes 1843204

commit v3 on v2

--- a/solution.py
+++ b/solution.py
@@ -180,17 +180,19 @@
     )(blocks, row_emb, col_emb)
 
 
-def merge_kernel(scale, plan, live, blocks, gain, offset, table, row_part, col_part, row_sum, seen):
+def merge_kernel(
+    scale, plan, live, blocks, gain, offset, table, row_part, col_part, row_sum, col_sum, seen
+):
     slots, sub_rows, sub_cols = blocks.shape
     places = table.shape[0]
     grid_columns = col_part.shape[0]
 
-    @pl.loop(0, places)
+    @pl.loop(0, places, unroll=8)
     def _(b):
         table[b] = slots
 
     row_sum[...] = jnp.zeros_like(row_sum)
-    col_part[...] = jnp.zeros_like(col_part)
+    col_sum[...] = jnp.zeros_like(col_sum)
     gain[slots] = jnp.zeros((sub_rows, sub_cols), jnp.float32)
     offset[slots] = jnp.zeros((sub_rows, sub_cols), jnp.float32)
 
@@ -202,27 +204,15 @@
             i = place // grid_columns
             j = place - i * grid_columns
             block = blocks[k]
-            row_sum[i] = row_sum[i] + block
-            col_part[pl.ds(j, 1), :] += jnp.sum(block, axis=0, keepdims=True)
             first = table[place]
             fresh = first == slots
             target = jnp.where(fresh, k, first)
             table[place] = target
-
-            @pl.when(fresh)
-            def _():
-                seen[k] = block
-
-            @pl.when(jnp.logical_not(fresh))
-            def _():
-                seen[target] = seen[target] + block
-                seen[k] = block
-
-        @pl.when(live[k] <= 0)
-        def _():
-            seen[k] = jnp.ones((sub_rows, sub_cols), jnp.float32)
-
-    @pl.loop(0, slots)
+            row_sum[i] = row_sum[i] + block
+            col_sum[j] = col_sum[j] + jnp.sum(block.reshape(sub_rows // 8, 8, sub_cols), axis=0)
+            seen[target] = jnp.where(fresh, block, seen[target] + block)
+
+    @pl.loop(0, slots, unroll=4)
     def _(k):
         counts = seen[k]
         confidence = scale * (0.1 + 0.25 * jnp.sqrt(counts))
@@ -230,6 +220,7 @@
         offset[k] = -confidence * jnp.log(counts)
 
     row_part[...] = jnp.sum(row_sum[...], axis=2)
+    col_part[...] = jnp.sum(col_sum[...], axis=1)
 
 
 def merge(scale, plan, live, blocks, grid_rows, grid_columns):
@@ -250,6 +241,7 @@
         out_specs=(vmem, vmem, smem, vmem, vmem),
         scratch_shapes=[
             pltpu.VMEM((grid_rows, sub_rows, sub_cols), f32),
+            pltpu.VMEM((grid_columns, 8, sub_cols), f32),
             pltpu.VMEM((slots, sub_rows, sub_cols), f32),
         ],
         compiler_params=pltpu.CompilerParams(vmem_limit_bytes=VMEM_LIMIT),
@@ -257,111 +249,13 @@
     )(plan, live, blocks)
 
 
-def mass_kernel(
-    n_row, n_col, row_part, col_part, row_log, col_log, row_in, col_in, tot_out, tot_in,
-    r_send, r_recv, c_send, c_recv, t_send, t_recv,
-):
-    r = lax.axis_index("row")
-    c = lax.axis_index("col")
-
-    def row_peer(k):
-        return (lax.rem(r + k, n_row), c)
-
-    def col_peer(k):
-        return (r, lax.rem(c + k, n_col))
-
-    barrier = pltpu.get_barrier_semaphore()
-
-    @pl.loop(1, n_row)
-    def _(k):
-        pl.semaphore_signal(barrier, inc=1, device_id=row_peer(k), device_id_type=MESH)
-
-    @pl.loop(1, n_col)
-    def _(k):
-        pl.semaphore_signal(barrier, inc=1, device_id=col_peer(k), device_id_type=MESH)
-
-    pl.semaphore_wait(barrier, n_row + n_col - 2)
-
-    def col_copy(k):
-        return remote(col_part, col_in.at[k], c_send.at[k], c_recv.at[k], row_peer(k))
-
-    def row_copy(k):
-        return remote(row_part, row_in.at[k], r_send.at[k], r_recv.at[k], col_peer(k))
-
-    def tot_copy(k):
-        return remote(tot_out, tot_in.at[k], t_send.at[k], t_recv.at[k], col_peer(k))
-
-    @pl.loop(1, n_row)
-    def _(k):
-        col_copy(k).start()
-
-    @pl.loop(1, n_col)
-    def _(k):
-        row_copy(k).start()
-
-    @pl.loop(1, n_row)
-    def _(k):
-        col_copy(k).wait()
-
-    col_mass = col_part[...]
-    for k in range(1, n_row):
-        col_mass = col_mass + col_in[k]
-    part = jnp.sum(jnp.sum(col_mass, axis=0, keepdims=True), axis=1, keepdims=True)
-    tot_out[...] = jnp.broadcast_to(part, tot_out.shape)
-
-    @pl.loop(1, n_col)
-    def _(k):
-        tot_copy(k).start()
-
-    @pl.loop(1, n_col)
-    def _(k):
-        row_copy(k).wait()
-
-    row_mass = row_part[...]
-    for k in range(1, n_col):
-        row_mass = row_mass + row_in[k]
-    row_log[...] = jnp.log(row_mass)
-
-    @pl.loop(1, n_col)
-    def _(k):
-        tot_copy(k).wait()
-
-    grand = tot_out[...]
-    for k in range(1, n_col):
-        grand = grand + tot_in[k]
-    col_log[...] = jnp.log(col_mass) - jnp.log(grand[0:1, :])
-
-
-def masses(n_row, n_col, row_part, col_part):
-    f32 = jnp.float32
-    vmem = pl.BlockSpec(memory_space=pltpu.VMEM)
-    dma = pltpu.SemaphoreType.DMA
-    return pl.pallas_call(
-        functools.partial(mass_kernel, n_row, n_col),
-        out_shape=(
-            jax.ShapeDtypeStruct(row_part.shape, f32),
-            jax.ShapeDtypeStruct(col_part.shape, f32),
-        ),
-        in_specs=[vmem] * 2,
-        out_specs=(vmem,) * 2,
-        scratch_shapes=[
-            pltpu.VMEM((n_col,) + row_part.shape, f32),
-            pltpu.VMEM((n_row,) + col_part.shape, f32),
-            pltpu.VMEM((8, col_part.shape[1]), f32),
-            pltpu.VMEM((n_col, 8, col_part.shape[1]), f32),
-            dma((n_col,)), dma((n_col,)), dma((n_row,)), dma((n_row,)), dma((n_col,)), dma((n_col,)),
-        ],
-        compiler_params=pltpu.CompilerParams(collective_id=1, has_side_effects=True),
-        name="masses",
-    )(row_part, col_part)
-
-
 def gradient_kernel(
     n_row, n_col, dim, dim_pad, depth, half_scale,
-    table, rows, cols, gain, offset, row_log, col_log, row_share, col_share,
+    table, rows, cols, gain, offset, row_part, col_part, row_share, col_share,
+    row_log, col_log, mass_row, mass_col, mass_out, mass_tot,
     pad_row, pad_col, row_left, row_turned, right_0, right_1, score_0, score_1, lg_hi, lg_lo,
     row_sum, col_out, pair_in, chip_in, row_in,
-    p_send, p_recv, h_send, h_recv, r_send, r_recv,
+    p_send, p_recv, h_send, h_recv, r_send, r_recv, mr_send, mr_recv, mc_send, mc_recv, mt_send, mt_recv,
 ):
     f32 = jnp.float32
     bf16 = jnp.bfloat16
@@ -381,17 +275,28 @@
     shard_lines = row_width // sub_rows
 
     barrier = pltpu.get_barrier_semaphore()
-    pl.semaphore_signal(barrier, inc=1, device_id=(sibling, c), device_id_type=MESH)
-
-    @pl.loop(1, chips)
-    def _(t):
-        pl.semaphore_signal(barrier, inc=1, device_id=(lax.rem(r + 2 * t, n_row), c), device_id_type=MESH)
+    def row_peer(k):
+        return (lax.rem(r + k, n_row), c)
+
+    def col_peer(k):
+        return (r, lax.rem(c + k, n_col))
+
+    @pl.loop(1, n_row)
+    def _(k):
+        pl.semaphore_signal(barrier, inc=1, device_id=row_peer(k), device_id_type=MESH)
 
     @pl.loop(1, n_col)
     def _(k):
-        pl.semaphore_signal(barrier, inc=1, device_id=(r, lax.rem(c + k, n_col)), device_id_type=MESH)
-
-    pl.semaphore_wait(barrier, chips + n_col - 1)
+        pl.semaphore_signal(barrier, inc=1, device_id=col_peer(k), device_id_type=MESH)
+
+    def col_mass_copy(k):
+        return remote(col_part, mass_col.at[k], mc_send.at[k], mc_recv.at[k], row_peer(k))
+
+    def row_mass_copy(k):
+        return remote(row_part, mass_row.at[k], mr_send.at[k], mr_recv.at[k], col_peer(k))
+
+    def tot_copy(k):
+        return remote(mass_out, mass_tot.at[k], mt_send.at[k], mt_recv.at[k], col_peer(k))
 
     def pair_copy(t):
         return remote(col_out.at[2 * t], pair_in.at[t], p_send.at[t], p_recv.at[t], (sibling, c))
@@ -469,6 +374,16 @@
     right_1[...] = jnp.zeros_like(right_1)
     row_sum[...] = jnp.zeros_like(row_sum)
 
+    pl.semaphore_wait(barrier, n_row + n_col - 2)
+
+    @pl.loop(1, n_row)
+    def _(k):
+        col_mass_copy(k).start()
+
+    @pl.loop(1, n_col)
+    def _(k):
+        row_mass_copy(k).start()
+
     @pl.loop(0, 2 * chips)
     def _(step):
         col_out[step] = jnp.zeros(col_out.shape[1:], f32)
@@ -484,7 +399,45 @@
             row_left[h, 2 * dim_pad : 3 * dim_pad, span] = high[:, part]
             row_turned[h, span, :] = row_left[h, :, span].T
 
+    @pl.loop(1, n_row)
+    def _(k):
+        col_mass_copy(k).wait()
+
+    col_mass = col_part[...]
+    for k in range(1, n_row):
+        col_mass = col_mass + mass_col[k]
+    part = jnp.sum(jnp.sum(col_mass, axis=0, keepdims=True), axis=1, keepdims=True)
+    mass_out[...] = jnp.broadcast_to(part, mass_out.shape)
+
+    @pl.loop(1, n_col)
+    def _(k):
+        tot_copy(k).start()
+
     prepare(0, 0, right_0, score_0)
+
+    @pl.loop(1, n_col)
+    def _(k):
+        row_mass_copy(k).wait()
+
+    row_mass = row_part[...]
+    for k in range(1, n_col):
+        row_mass = row_mass + mass_row[k]
+    logs = jnp.log(row_mass)
+    square = (sub_rows, sub_rows)
+    diagonal = lax.broadcasted_iota(jnp.int32, square, 0) == lax.broadcasted_iota(jnp.int32, square, 1)
+    for i in range(logs.shape[0]):
+        spread = jnp.where(diagonal, jnp.broadcast_to(logs[i : i + 1, :], square), 0.0)
+        column = jnp.sum(spread, axis=1, keepdims=True)
+        row_log[i * sub_rows : (i + 1) * sub_rows, :] = jnp.broadcast_to(column, (sub_rows, sub_cols))
+
+    @pl.loop(1, n_col)
+    def _(k):
+        tot_copy(k).wait()
+
+    grand = mass_out[...]
+    for k in range(1, n_col):
+        grand = grand + mass_tot[k]
+    col_log[...] = jnp.log(col_mass) - jnp.log(grand[0:1, :])
 
     @pl.loop(0, halves * chips)
     def _(u):
@@ -542,7 +495,7 @@
             row_copy(h, k).wait_send()
 
 
-def gradients(n_row, n_col, half_scale, table, rows, cols, gain, offset, row_log, col_log):
+def gradients(n_row, n_col, half_scale, table, rows, cols, gain, offset, row_part, col_part):
     f32 = jnp.float32
     bf16 = jnp.bfloat16
     dim, row_width = rows.shape[1:]
@@ -552,6 +505,8 @@
     halves = 2 if row_width % 256 == 0 else 1
     piece = row_width // halves
     half_rows = n_col * piece
+    tile_rows = n_col * row_width
+    sub_cols = gain.shape[2]
     chips = n_row // 2
     smem = pl.BlockSpec(memory_space=pltpu.SMEM)
     vmem = pl.BlockSpec(memory_space=pltpu.VMEM)
@@ -565,6 +520,12 @@
         in_specs=[smem] + [vmem] * 6,
         out_specs=(vmem,) * 2,
         scratch_shapes=[
+            pltpu.VMEM((tile_rows, sub_cols), f32),
+            pltpu.VMEM(col_part.shape, f32),
+            pltpu.VMEM((n_col,) + row_part.shape, f32),
+            pltpu.VMEM((n_row,) + col_part.shape, f32),
+            pltpu.VMEM((8, sub_cols), f32),
+            pltpu.VMEM((n_col, 8, sub_cols), f32),
             pltpu.VMEM((dim_pad, row_width), f32),
             pltpu.VMEM((dim_pad, col_width), f32),
             pltpu.VMEM((halves, depth, half_rows), bf16),
@@ -582,12 +543,13 @@
             pltpu.VMEM((halves, n_col, dim_pad, piece), f32),
             dma((chips,)), dma((chips,)), dma((chips,)), dma((chips,)),
             dma((halves * n_col,)), dma((halves * n_col,)),
+            dma((n_col,)), dma((n_col,)), dma((n_row,)), dma((n_row,)), dma((n_col,)), dma((n_col,)),
         ],
         compiler_params=pltpu.CompilerParams(
-            collective_id=2, has_side_effects=True, vmem_limit_bytes=VMEM_LIMIT
+            collective_id=1, has_side_effects=True, vmem_limit_bytes=VMEM_LIMIT
         ),
         name="gradients",
-    )(table, rows, cols, gain, offset, row_log, col_log)
+    )(table, rows, cols, gain, offset, row_part, col_part)
 
 
 def per_device(blocks, plan, live, row_emb, col_emb, row_acc, col_acc):
@@ -605,10 +567,8 @@
         scale, places.reshape(-1), alive.reshape(-1), arrived.reshape(-1, sub_rows, sub_cols),
         tile_rows // sub_rows, tile_cols // sub_cols,
     )
-    row_log, col_log = masses(n_row, n_col, row_part, col_part)
-    row_wide = jnp.broadcast_to(row_log.reshape(tile_rows, 1), (tile_rows, sub_cols))
     row_share, col_share = gradients(
-        n_row, n_col, 0.5 * scale, table, rows, cols, gain, offset, row_wide, col_log
+        n_row, n_col, 0.5 * scale, table, rows, cols, gain, offset, row_part, col_part
     )
     new_row_acc = row_acc + row_share * row_share
     new_col_acc = col_acc + col_share * col_share

time: 175 us -> 164 us (0.937)
  Pallas kernels: 163 us -> 155 us
  local copies, waits for them, and re-layouts: 3.82 us -> 2.01 us
    pallas_call x1 -> x0, Pallas kernels: 12 us -> none  [masses(): pl.pallas_call(functools.partial(mass_kernel, n_row, n_col), out_shape=(j...]
    pallas_call x1, Pallas kernels: 58.5 us -> 65.7 us  [gradients(): pl.pallas_call(functools.partial(gradient_kernel, n_row, n_col, dim, dim_...]
    pallas_call x1, Pallas kernels: 10.9 us -> 7.07 us  [merge(): pl.pallas_call(functools.partial(merge_kernel, scale), out_shape=(jax.Sha...]
    broadcast_in_dim x2 -> x0, local copies, waits for them, and re-layouts: 1.76 us -> none  [per_device(): jnp.broadcast_to(row_log.reshape(tile_rows, 1), (tile_rows, sub_cols))]
where the time goes in v3:
time: 164 us; the launch traced here: 162 us
  Pallas kernels  155 us (95%)
  other arithmetic  4.91 us (3%)
  local copies, waits for them, and re-layouts  2.01 us (1%)
    pallas_call x1, Pallas kernels, exchange(): pl.pallas_call(functools.partial(exchange_kernel, n_row, n_col), out_shap...  81.9 us
    pallas_call x1, Pallas kernels, gradients(): pl.pallas_call(functools.partial(gradient_kernel, n_row, n_col, dim, dim_...  65.7 us
    pallas_call x1, Pallas kernels, merge(): pl.pallas_call(functools.partial(merge_kernel, scale), out_shape=(jax.Sha...  7.07 us

profile of v3, /device:TPU:0, one launch (start us, length us, event | category | flops | bytes accessed | tf_op | source)
XLA Modules:
  0.0 162.3 jit_solution(3852298373075253938)
XLA Ops:
  0.6 0.8 copy.12
  1.4 0.6 reshape_squeeze.3.plan
  2.0 0.8 fusion
  2.8 0.6 reshape.19.live
  3.4 81.9 %exchange.1 = (f32[4,8,2,64,128]{4,3,2,1,0:T(8,128)}, f32[4,300,256]{2,1,0:T(8,128)}, f32[8,300,512]{2,1,0:T(8,128)}) custom-call(f32[4,8,2,64,128]{4,3,2,1,0:T(8,128)} %bitcast.5, f32[300,256]{1,0:T(8,128)} %row_emb.1, f32[300,512]{1,0:T(8,128)} %col_emb.1), custom_call_target="tpu_custom_call" | custom-call | tf_op jit(solution)/shard_map/exchange/pallas_call | solution.py:165
  85.3 7.1 %merge.1 = (f32[65,64,128]{2,1,0:T(8,128)}, f32[65,64,128]{2,1,0:T(8,128)}, s32[512]{0:T(512)}, f32[16,64]{1,0:T(8,128)}, f32[32,128]{1,0:T(8,128)}) custom-call(s32[64]{0:T(128)} %reshape_squeeze.3.plan, s32[64]{0:T(128)} %reshape.19.live, f32[64,64,128]{2,1,0:T(8,128)} %bitcast.6), custom_call_target="tpu_custom_call" | custom-call | tf_op jit(solution)/shard_map/merge/pallas_call | solution.py:231
  92.4 0.0 copy-start.1
  92.4 0.0 copy-start.3
  92.4 0.0 copy-start
  92.4 0.0 copy-start.2
  92.4 65.7 %gradients.1 = (f32[300,256]{1,0:T(8,128)}, f32[300,512]{1,0:T(8,128)}) custom-call(s32[512]{0:T(512)} %get-tuple-element.15.table, f32[4,300,256]{2,1,0:T(8,128)} %get-tuple-element.16.rows, f32[8,300,512]{2,1,0:T(8,128)} %get-tuple-element.17.cols, f32[65,64,128]{2,1,0:T(8,128)} %get-tuple-element.18.gain, f32[65,64,128]{2,1,0:T(8,128)} %get-tuple-element.19.offset, ...), custom_call_target="tpu_custom_call" | custom-call | tf_op jit(solution)/shard_map/gradients/pallas_call | solution.py:514
  158.2 0.0 copy-done.1
  158.2 0.0 copy-done.3
  158.2 1.9 %multiply_subtract_fusion.1 = (f32[300,256]{1,0:T(8,128)}, f32[300,256]{1,0:T(8,128)}) fusion(f32[300,256]{1,0:T(8,128)S(1)} %copy-done.1, f32[300,256]{1,0:T(8,128)} %get-tuple-element.22, f32[300,256]{1,0:T(8,128)S(1)} %copy-done.3), kind=kLoop, calls=%fused_computation.2 | loop fusion | flops 384000 | bytes 1536000 | tf_op jit(solution)/shard_map/sub | solution.py:575
  160.0 0.0 copy-done
  160.0 0.0 copy-done.2
  160.0 2.3 %multiply_subtract_fusion = (f32[300,512]{1,0:T(8,128)}, f32[300,512]{1,0:T(8,128)}) fusion(f32[300,512]{1,0:T(8,128)S(1)} %copy-done, f32[300,512]{1,0:T(8,128)} %get-tuple-element.23, f32[300,512]{1,0:T(8,128)S(1)} %copy-done.2), kind=kLoop, calls=%fused_computation | loop fusion | flops 768000 | bytes 3072000 | tf_op jit(solution)/shard_map/sub | solution.py:576
Async XLA Ops:
  92.4 65.8 %copy-start.1 = (f32[300,256]{1,0:T(8,128)S(1)}, f32[300,256]{1,0:T(8,128)}, u32[]{:S(2)}) copy-start(f32[300,256]{1,0:T(8,128)} %row_emb.1) | copy-start | bytes 921604
  92.4 65.8 %copy-start.3 = (f32[300,256]{1,0:T(8,128)S(1)}, f32[300,256]{1,0:T(8,128)}, u32[]{:S(2)}) copy-start(f32[300,256]{1,0:T(8,128)} %param.12) | copy-start | bytes 921604
  92.4 67.6 %copy-start = (f32[300,512]{1,0:T(8,128)S(1)}, f32[300,512]{1,0:T(8,128)}, u32[]{:S(2)}) copy-start(f32[300,512]{1,0:T(8,128)} %col_emb.1) | copy-start | bytes 1843204
  92.4 67.6 %copy-start.2 = (f32[300,512]{1,0:T(8,128)S(1)}, f32[300,512]{1,0:T(8,128)}, u32[]{:S(2)}) copy-start(f32[300,512]{1,0:T(8,128)} %param.13) | copy-start | bytes 1843204
